TPU v7x, 512 devices: a whole 4x8x8 slice. The times are simulated.
512 devices in a mesh: adapter: 64 (over z, x, core), tensor: 8 (over y).
Axes of the slice: x: 4, y: 8, z: 8, core: 2. Of those that a mesh axis runs over, the one named last changes fastest.
Arguments:
- tokens: bfloat16 [8192, 8192], P('adapter', 'tensor'), may hold values from -6 to 6
- token_adapter_index: int32 [8192, 1], P('adapter'), may hold values from 0 to 127; in each aligned block of 128 rows (0 to 127, 128 to 255, ...) at most 3 rows name the same one
- key_value_weight: bfloat16 [8192, 2, 1024], P('tensor'), may hold values from -0.0625 to 0.0625
- adapter_down_weight: bfloat16 [128, 8192, 128], P('adapter', 'tensor'), may hold values from -0.0625 to 0.0625
- adapter_up_query: bfloat16 [128, 64, 8192], P('adapter', None, 'tensor'), may hold values from -0.75 to 0.75
- adapter_up_value: bfloat16 [128, 64, 1024], P('adapter', None, 'tensor'), may hold values from -0.75 to 0.75
Outputs:
- q_delta: bfloat16 [8192, 8192], P('adapter', 'tensor')
- keys: bfloat16 [8192, 1024], P('adapter', 'tensor')
- values: bfloat16 [8192, 1024], P('adapter', 'tensor')
Inputs may be any that keep to these rules, and one draw needn't show every extreme that they name: `token_adapter_index`: among the 128 tokens of one index of the adapter axis no adapter occurs more than 3 times.
All inputs are finite; a program needn't handle non-finite values.
Results may differ from a plain program's by a relative error of at most 0.0049.
Values may be sent and summed in bfloat16 or wider, within the bound.
A program may use at most 64 MiB of HBM per device.

v0:
```python
import jax
import jax.numpy as jnp
from jax import lax
from jax.sharding import PartitionSpec as P


def local(
    tokens,
    token_adapter_index,
    key_value_weight,
    adapter_down_weight,
    adapter_up_query,
    adapter_up_value,
):
    tok_rows, features = tokens.shape
    holders = lax.axis_size("adapter")
    per_shard_count = adapter_down_weight.shape[0]
    rank_length = adapter_down_weight.shape[2] // 2
    most_rows = 3 * tok_rows // (per_shard_count * holders)
    slots_all = holders * per_shard_count * most_rows
    query_feature_width = adapter_up_query.shape[2]
    head_width = key_value_weight.shape[2]
    adapter_of = token_adapter_index[:, 0]
    matching = adapter_of[:, None] == adapter_of[None, :]
    earlier = lax.broadcasted_iota(jnp.int32, (tok_rows, tok_rows), 0) > lax.broadcasted_iota(
        jnp.int32, (tok_rows, tok_rows), 1
    )
    ordinal = jnp.sum((matching & earlier).astype(jnp.int32), axis=1)
    slot_of = adapter_of * most_rows + ordinal
    source_row = (
        jnp.zeros((slots_all,), jnp.int32).at[slot_of].set(jnp.arange(tok_rows, dtype=jnp.int32))
    )
    filled = jnp.zeros((slots_all,), jnp.bool_).at[slot_of].set(True)
    outgoing = jnp.where(filled[:, None], tokens[source_row], jnp.zeros((), jnp.bfloat16))
    outgoing = outgoing.reshape(holders, per_shard_count, most_rows, features)
    flat_weight = key_value_weight.reshape(features, 2 * head_width)
    base_terms = jnp.dot(tokens, flat_weight, preferred_element_type=jnp.float32).reshape(
        tok_rows, 2, head_width
    )
    base_heads = lax.psum_scatter(base_terms, "tensor", scatter_dimension=2, tiled=True)
    received_rows = lax.all_to_all(outgoing, "adapter", split_axis=0, concat_axis=0, tiled=True)
    partial_value = jnp.einsum(
        "exht,xto->exho", received_rows, adapter_down_weight, preferred_element_type=jnp.float32
    )
    reduced_hidden = lax.psum(partial_value, "tensor").astype(jnp.bfloat16)
    delta_q = jnp.einsum(
        "gxfe,xeb->gxfb",
        reduced_hidden[..., :rank_length],
        adapter_up_query,
        preferred_element_type=jnp.float32,
    )
    delta_v = jnp.einsum(
        "gxfe,xeb->gxfb",
        reduced_hidden[..., rank_length:],
        adapter_up_value,
        preferred_element_type=jnp.float32,
    )
    returned = lax.all_to_all(
        jnp.concatenate([delta_q, delta_v], axis=3).astype(jnp.bfloat16),
        "adapter",
        split_axis=0,
        concat_axis=0,
        tiled=True,
    )
    flat_back = returned.reshape(slots_all, returned.shape[3])
    per_token = flat_back[slot_of]
    q_delta = per_token[:, :query_feature_width]
    keys = base_heads[:, 0, :].astype(jnp.bfloat16)
    values = (base_heads[:, 1, :] + per_token[:, query_feature_width:].astype(jnp.float32)).astype(
        jnp.bfloat16
    )
    return (q_delta, keys, values)


def solution(mesh):
    placed = (
        P("adapter", "tensor"),
        P("adapter", None),
        P("tensor", None, None),
        P("adapter", "tensor", None),
        P("adapter", None, "tensor"),
        P("adapter", None, "tensor"),
    )
    return jax.shard_map(
        local,
        mesh=mesh,
        in_specs=placed,
        out_specs=(P("adapter", "tensor"), P("adapter", "tensor"), P("adapter", "tensor")),
        check_vma=False,
    )
```

profile of v0, /device:TPU:1, one launch (start us, length us, event | category | flops | bytes accessed | tf_op | source)
XLA Modules:
  0.0 133.9 jit_solution(4689913751884479216)
XLA Ops:
  7.2 0.9 convert_reduce_fusion
  8.1 0.7 fusion.18
  8.8 1.0 scatter_custom_fusion.1
  9.8 3.8 %gather_fusion = bf16[384,1024]{1,0:T(8,128)(2,1)S(1)} fusion(bf16[128,1024]{1,0:T(8,128)(2,1)} %param.6, s32[1024]{0:T(1024)S(1)} %pad_clamp_fusion.1), kind=kCustom, calls=%fused_computation | custom fusion | bytes 1574400 | tf_op jit(solution)/shard_map/gather | solution.py:34
  13.5 0.5 gather.9
  14.0 1.0 scatter_custom_fusion
  15.3 0.6 broadcast_select_fusion
  15.9 1.6 %copy.22 = bf16[64,2,3,1024]{3,1,2,0:T(2,128)(2,1)} copy(bf16[64,2,3,1024]{3,2,1,0:T(4,128)(2,1)S(1)} %broadcast_select_fusion) | data formatting | bytes 1572864 | tf_op jit(solution)/shard_map/jit(_where)/select_n | solution.py:34
  17.5 14.8 %all-to-all-start = ((bf16[64,2,3,1024]{3,1,2,0:T(2,128)(2,1)}), bf16[64,2,3,1024]{3,1,2,0:T(2,128)(2,1)S(1)}, u32[]{:S(2)}, u32[]{:S(2)}) async-start(bf16[64,2,3,1024]{3,1,2,0:T(2,128)(2,1)} %copy.22), calls=%async_computation | async-start | bytes 1572864 | tf_op jit(solution)/shard_map/all_to_all | solution.py:41
  32.4 5.6 %copy.30 = bf16[128,8,2,1024]{3,1,2,0:T(8,128)(2,1)} copy(bf16[128,8,2,1024]{3,2,1,0:T(2,128)(2,1)} %bitcast.47) | data formatting | bytes 8388608
  38.0 6.4 %copy.26 = bf16[2048,1024]{1,0:T(8,128)(2,1)} copy(bf16[2048,1024]{0,1:T(8,128)(2,1)} %bitcast.46) | data formatting | bytes 8388608 | tf_op jit(solution)/shard_map/dot_general | solution.py:37
  44.4 4.7 %fusion.5 = f32[128,2,1024]{2,0,1:T(8,128)} fusion(bf16[2,1024,1024]{2,1,0:T(8,128)(2,1)} %bitcast.45, bf16[128,1024]{1,0:T(8,128)(2,1)S(1)} %copy-done.1), kind=kOutput, calls=%fused_computation.14 | convolution fusion | flops 536870912 | bytes 5505024 | tf_op jit(solution)/shard_map/dot_general | solution.py:37
  49.2 5.9 %all-to-all-done = bf16[64,2,3,1024]{3,1,2,0:T(2,128)(2,1)S(1)} async-done(((bf16[64,2,3,1024]{3,1,2,0:T(2,128)(2,1)}), bf16[64,2,3,1024]{3,1,2,0:T(2,128)(2,1)S(1)}, u32[]{:S(2)}, u32[]{:S(2)}) %all-to-all-start) | async-done | bytes 786464 | tf_op jit(solution)/shard_map/all_to_all | solution.py:41
  55.1 0.4 convolution_bitcast_fusion
  55.5 27.9 %all-reduce.1 = bf16[64,2,3,128]{3,0,2,1:T(8,128)(2,1)S(1)} all-reduce(f32[64,2,3,128]{3,0,2,1:T(8,128)S(1)} %convolution_bitcast_fusion), channel_id=1, replica_groups=mesh['adapter'=64,'tensor'=8] {'tensor'}, use_global_device_ids=true, to_apply=%region_3.4 | all-reduce | flops 49152 | bytes 294912 | tf_op jit(solution)/shard_map/psum | solution.py:45
  84.1 1.8 %copy.24 = bf16[64,2,3,1152]{3,1,2,0:T(2,128)(2,1)} copy(bf16[64,2,3,1152]{3,0,2,1:T(8,128)(2,1)S(1)} %pad_maximum_fusion) | data formatting | bytes 1769472 | tf_op jit(solution)/shard_map/concatenate | solution.py:59
  86.0 12.9 %all-to-all-start.1 = ((bf16[64,2,3,1152]{3,1,2,0:T(2,128)(2,1)}), bf16[64,2,3,1152]{3,1,2,0:T(2,128)(2,1)S(1)}, u32[]{:S(2)}, u32[]{:S(2)}) async-start(bf16[64,2,3,1152]{3,1,2,0:T(2,128)(2,1)} %copy.24), calls=%async_computation.1 | async-start | bytes 1769472 | tf_op jit(solution)/shard_map/all_to_all | solution.py:58
  98.9 1.5 %fusion.12 = bf16[128,128]{1,0:T(8,128)(2,1)} fusion(f32[128,2,128]{2,0,1:T(8,128)} %reduce-scatter.2.cloned.1.call-done), kind=kLoop, calls=%fused_computation.25 | loop fusion | bytes 65536 | tf_op jit(solution)/shard_map/convert_element_type | solution.py:68
  100.3 23.1 %all-to-all-done.1 = bf16[64,2,3,1152]{3,1,2,0:T(2,128)(2,1)S(1)} async-done(((bf16[64,2,3,1152]{3,1,2,0:T(2,128)(2,1)}), bf16[64,2,3,1152]{3,1,2,0:T(2,128)(2,1)S(1)}, u32[]{:S(2)}, u32[]{:S(2)}) %all-to-all-start.1) | async-done | bytes 884768 | tf_op jit(solution)/shard_map/all_to_all | solution.py:58
  123.5 0.5 copy.25
  124.0 0.8 reshape.25
  124.7 0.9 gather_fusion.1
  125.7 0.7 slice.31
  126.4 0.6 fusion.10
  (22 shorter events, 1.0 us)
Async XLA Ops:
  7.2 47.9 %copy-start = (bf16[2,1024,128]{2,1,0:T(8,128)(2,1)S(1)}, bf16[2,1024,128]{2,1,0:T(8,128)(2,1)}, u32[]{:S(2)}) copy-start(bf16[2,1024,128]{2,1,0:T(8,128)(2,1)} %param.9) | copy-start | bytes 1572868
  17.5 37.6 %all-to-all-start = ((bf16[64,2,3,1024]{3,1,2,0:T(2,128)(2,1)}), bf16[64,2,3,1024]{3,1,2,0:T(2,128)(2,1)S(1)}, u32[]{:S(2)}, u32[]{:S(2)}) async-start(bf16[64,2,3,1024]{3,1,2,0:T(2,128)(2,1)} %copy.22), calls=%async_computation | async-start | bytes 1572864 | tf_op jit(solution)/shard_map/all_to_all | solution.py:41
  32.4 66.5 %reduce-scatter.2.cloned.1.call-start = ((), (), s32[]{:S(2)}) async-start(), calls=%async_computation.3 | async-start | bytes 1179648 | tf_op jit(solution)/shard_map/reduce_scatter | solution.py:40
  38.0 6.4 %copy-start.1 = (bf16[128,1024]{1,0:T(8,128)(2,1)S(1)}, bf16[128,1024]{1,0:T(8,128)(2,1)}, u32[]{:S(2)}) copy-start(bf16[128,1024]{1,0:T(8,128)(2,1)} %param.6) | copy-start | bytes 786436
  44.4 39.0 %copy-start.4 = (bf16[2,64,128]{2,1,0:T(8,128)(2,1)S(1)}, bf16[2,64,128]{2,1,0:T(8,128)(2,1)}, u32[]{:S(2)}) copy-start(bf16[2,64,128]{2,1,0:T(8,128)(2,1)} %param.11) | copy-start | bytes 98308
  44.4 39.2 %copy-start.2 = (bf16[2,64,1024]{2,1,0:T(8,128)(2,1)S(1)}, bf16[2,64,1024]{2,1,0:T(8,128)(2,1)}, u32[]{:S(2)}) copy-start(bf16[2,64,1024]{2,1,0:T(8,128)(2,1)} %param.10) | copy-start | bytes 786436
  86.0 37.5 %all-to-all-start.1 = ((bf16[64,2,3,1152]{3,1,2,0:T(2,128)(2,1)}), bf16[64,2,3,1152]{3,1,2,0:T(2,128)(2,1)S(1)}, u32[]{:S(2)}, u32[]{:S(2)}) async-start(bf16[64,2,3,1152]{3,1,2,0:T(2,128)(2,1)} %copy.24), calls=%async_computation.1 | async-start | bytes 1769472 | tf_op jit(solution)/shard_map/all_to_all | solution.py:58
  123.9 2.4 %copy-start.3 = (f32[128,2,128]{2,0,1:T(8,128)S(1)}, f32[128,2,128]{2,0,1:T(8,128)}, u32[]{:S(2)}) copy-start(f32[128,2,128]{2,0,1:T(8,128)} %reduce-scatter.2.cloned.1.call-done) | copy-start | bytes 393220
Sparse Core Ops, SparseCore 0:
  49.3 38.9 reduce-scatter.1
where the time goes:
time: 134 us
  waiting for transfers between devices  29.1 us (22%)
  blocking collectives  27.9 us (21%)
  starting transfers between devices  27.7 us (21%)
  local copies, waits for them, and re-layouts  26.3 us (20%)
  between operations  14.2 us (11%)
  matrix products  5.69 us (4%)
  other arithmetic  2.85 us (2%)
    psum x1, blocking collectives, local(): reduced_hidden = lax.psum(partial_value, 'tensor').astype(jnp.bfloat16)  27.9 us
    all_to_all x1, waiting for transfers between devices, local(): lax.all_to_all(jnp.concatenate([delta_q, delta_v], axis=3).astype(jnp.bfl...  23.1 us
    all_to_all x1, starting transfers between devices, local(): lax.all_to_all(outgoing, 'adapter', split_axis=0, concat_axis=0, tiled=True)  14.8 us
    all_to_all x1, starting transfers between devices, local(): lax.all_to_all(jnp.concatenate([delta_q, delta_v], axis=3).astype(jnp.bfl...  12.9 us
    dot_general x1, local copies, waits for them, and re-layouts, local(): jnp.dot(tokens, flat_weight, preferred_element_type=jnp.float32)  6.44 us
    all_to_all x1, waiting for transfers between devices, local(): lax.all_to_all(outgoing, 'adapter', split_axis=0, concat_axis=0, tiled=True)  5.92 us
    unnamed x11, local copies, waits for them, and re-layouts  5.61 us
    dot_general x1, matrix products, local(): jnp.dot(tokens, flat_weight, preferred_element_type=jnp.float32)  4.71 us
  transfers between devices with their start and end apart: 3, of which 2 were waited for; matrix products, arithmetic and copies ran while one was open for 16% of the time, Pallas kernels for 0%

commit v1 on v0

v1 whole, which is shorter than its diff:
```python
import functools
import jax
import jax.numpy as jnp
from jax import lax
from jax.experimental import pallas as pl
from jax.experimental.pallas import tpu as pltpu
from jax.sharding import PartitionSpec as P

MESH = pl.DeviceIdType.MESH
LANES = 128
BF16 = jnp.bfloat16
F32 = jnp.float32
MOST = 3
ZS, XS, CORES = 8, 4, 2
CHUNKS = 2


def kernel(
    holders,
    tensors,
    tok_hbm,
    idx_hbm,
    kvw_hbm,
    down_hbm,
    upq_hbm,
    upv_hbm,
    q_out,
    k_out,
    v_out,
    tok,
    idx,
    kvw,
    wbase,
    lhs,
    down,
    up,
    fsel,
    stage,
    send,
    recv,
    xs,
    part,
    rs,
    sh,
    ustage,
    ret_send,
    ret_recv,
    bs_send,
    bs_recv,
    load_sems,
    send_sems,
    recv_sems,
):
    me = lax.axis_index("adapter")
    t = lax.axis_index("tensor")
    rows, features = tok.shape
    blocks = features // LANES
    per_holder = down.shape[0]
    adapters = holders * per_holder
    tile = per_holder * blocks
    chunk = holders // CHUNKS
    z = me // (XS * CORES)
    x = (me // CORES) % XS
    core = me % CORES
    self_pos = z * CORES + core

    def peer_of(p):
        near = (p // (ZS * CORES)) % 2
        far = p // (2 * ZS * CORES)
        px = (x + near * (1 - 2 * (x % 2)) + 2 * far) % XS
        return ((p // CORES) % ZS) * (XS * CORES) + px * CORES + p % CORES

    def my_pos(p):
        return (p // (ZS * CORES)) * (ZS * CORES) + self_pos

    def position(k, d):
        return k * chunk + (self_pos + d) % chunk

    def for_peers(k, act):
        @pl.loop(1 if k == 0 else 0, chunk)
        def _(d):
            act(position(k, d))

    barrier = pltpu.get_barrier_semaphore()

    @pl.loop(1, tensors)
    def _(d):
        pl.semaphore_signal(barrier, inc=1, device_id=(me, (t + d) % tensors), device_id_type=MESH)

    @pl.loop(1, holders)
    def _(d):
        pl.semaphore_signal(barrier, inc=1, device_id=((me + d) % holders, t), device_id_type=MESH)

    get_tok = pltpu.make_async_copy(tok_hbm, tok, load_sems.at[0])
    get_idx = pltpu.make_async_copy(idx_hbm, idx, load_sems.at[1])
    get_kvw = pltpu.make_async_copy(kvw_hbm, kvw, load_sems.at[2])
    get_down = pltpu.make_async_copy(down_hbm, down, load_sems.at[3])
    get_idx.start()
    get_tok.start()
    get_kvw.start()
    get_down.start()

    get_idx.wait()
    lane = lax.broadcasted_iota(jnp.int32, (rows, adapters), 1)
    picked = (idx[...] == lane).astype(F32)
    earlier = lax.broadcasted_iota(jnp.int32, (rows, rows), 0) > lax.broadcasted_iota(
        jnp.int32, (rows, rows), 1
    )
    ordinal = jnp.dot(
        earlier.astype(F32).astype(BF16), picked.astype(BF16), preferred_element_type=F32
    )
    get_tok.wait()
    for m in range(MOST):
        chosen = jnp.where(ordinal == float(m), picked, 0.0)
        fsel[:, m * adapters : (m + 1) * adapters] = chosen.astype(BF16)
        gathered = jnp.dot(chosen.T.astype(BF16), tok[...], preferred_element_type=F32)
        for j in range(blocks):
            stage[m, pl.ds(j, adapters, stride=blocks), :] = gathered[:, j * LANES : (j + 1) * LANES]
        send[:, :, m * LANES : (m + 1) * LANES] = (
            stage[m].reshape(holders, tile, LANES).astype(BF16)
        )

    pl.semaphore_wait(barrier, tensors - 1 + holders - 1)

    def dispatch(k, p):
        return pltpu.make_async_remote_copy(
            src_ref=send.at[peer_of(p)],
            dst_ref=recv.at[my_pos(p)],
            send_sem=send_sems.at[0],
            recv_sem=recv_sems.at[k],
            device_id=(peer_of(p), t),
            device_id_type=MESH,
        )

    for k in range(CHUNKS):
        for_peers(k, lambda p, k=k: dispatch(k, p).start())
    recv[self_pos] = send[me]

    up[...] = jnp.zeros_like(up)
    get_ups = []
    for a in range(per_holder):
        rank = upq_hbm.shape[1]
        get_ups.append(
            pltpu.make_async_copy(
                upq_hbm.at[a], up.at[a, pl.ds(0, rank), pl.ds(0, features)], load_sems.at[4 + a]
            )
        )
        get_ups.append(
            pltpu.make_async_copy(
                upv_hbm.at[a],
                up.at[a, pl.ds(rank, rank), pl.ds(features, LANES)],
                load_sems.at[4 + per_holder + a],
            )
        )
    for copy in get_ups:
        copy.start()
    for c in range(2):
        spread = (
            lax.broadcasted_iota(jnp.int32, (LANES, 2 * LANES), 1)
            == 2 * lax.broadcasted_iota(jnp.int32, (LANES, 2 * LANES), 0) + c
        ).astype(F32).astype(BF16)
        for j in range(blocks):
            lhs[c, :, 2 * j * LANES : 2 * (j + 1) * LANES] = jnp.dot(
                tok[:, j * LANES : (j + 1) * LANES], spread, preferred_element_type=F32
            ).astype(BF16)
    get_kvw.wait()
    step = 32

    @pl.loop(0, features // step)
    def _(i):
        wbase[pl.ds(i * 2 * step, 2 * step), :] = kvw[pl.ds(i * step, step)].reshape(
            2 * step, wbase.shape[1]
        )

    @pl.loop(0, tensors // 2)
    def _(n):
        columns = pl.ds(pl.multiple_of(n * 2 * LANES, 2 * LANES), 2 * LANES)
        for c in range(2):
            terms = jnp.dot(lhs[c], wbase[:, columns], preferred_element_type=F32).astype(BF16)
            for half in range(2):
                bs_send[2 * n + half, :, c * LANES : (c + 1) * LANES] = terms[
                    :, half * LANES : (half + 1) * LANES
                ]

    def base_copy(d):
        other = (t + d) % tensors
        return pltpu.make_async_remote_copy(
            src_ref=bs_send.at[other],
            dst_ref=bs_recv.at[t],
            send_sem=send_sems.at[1],
            recv_sem=recv_sems.at[2],
            device_id=(me, other),
            device_id_type=MESH,
        )

    @pl.loop(1, tensors)
    def _(d):
        base_copy(d).start()

    bs_recv[t] = bs_send[t]
    ustage[MOST] = jnp.zeros_like(ustage[MOST])

    share = MOST * per_holder * chunk // tensors

    def partial(k):
        for m in range(MOST):
            stage[m, pl.ds(0, chunk * tile), :] = (
                recv[pl.ds(k * chunk, chunk), :, m * LANES : (m + 1) * LANES]
                .astype(F32)
                .reshape(chunk * tile, LANES)
            )
        for a in range(per_holder):
            for m in range(MOST):
                for j in range(blocks):
                    xs[a, m * chunk : (m + 1) * chunk, j * LANES : (j + 1) * LANES] = stage[
                        m, pl.ds(a * blocks + j, chunk, stride=tile), :
                    ].astype(BF16)
            terms = jnp.dot(xs[a], down[a], preferred_element_type=F32)
            owners = tensors // per_holder
            for s in range(owners):
                part[k, a * owners + s] = terms[s * share : (s + 1) * share]

        def scatter(d):
            other = (t + d) % tensors
            return pltpu.make_async_remote_copy(
                src_ref=part.at[k, other],
                dst_ref=rs.at[k, t],
                send_sem=send_sems.at[2],
                recv_sem=recv_sems.at[3 + k],
                device_id=(me, other),
                device_id_type=MESH,
            )

        @pl.loop(1, tensors)
        def _(d):
            scatter(d).start()

        rs[k, t] = part[k, t]

    def wait_bytes(ref, sem):
        pltpu.make_async_copy(ref, ref, sem).wait()

    def total(k):
        wait_bytes(rs.at[k, pl.ds(0, tensors - 1)], recv_sems.at[3 + k])
        summed = rs[k, 0]
        for s in range(1, tensors):
            summed = summed + rs[k, s]
        padded = jnp.concatenate([summed, jnp.zeros((sh.shape[2] - share, LANES), F32)], axis=0)
        sh[k, t] = padded.astype(BF16)

        def gather(d):
            return pltpu.make_async_remote_copy(
                src_ref=sh.at[k, t],
                dst_ref=sh.at[k, t],
                send_sem=send_sems.at[3],
                recv_sem=recv_sems.at[5 + k],
                device_id=(me, (t + d) % tensors),
                device_id_type=MESH,
            )

        @pl.loop(1, tensors)
        def _(d):
            gather(d).start()

    def corrections(k):
        wait_bytes(sh.at[k, pl.ds(0, tensors - 1)], recv_sems.at[5 + k])
        shrunk = sh[k].astype(F32)[:, :share].reshape(tensors * share, LANES).astype(BF16)
        each = MOST * chunk
        for a in range(per_holder):
            deltas = jnp.dot(
                shrunk[a * each : (a + 1) * each], up[a], preferred_element_type=F32
            )
            for m in range(MOST):
                of_m = deltas[m * chunk : (m + 1) * chunk]
                for j in range(blocks):
                    ustage[m, pl.ds(a * blocks + j, chunk, stride=tile), :] = of_m[
                        :, j * LANES : (j + 1) * LANES
                    ]
                ustage[MOST, pl.ds(a * blocks + m, chunk, stride=tile), :] = of_m[:, features:]
        for m in range(MOST + 1):
            ret_send[pl.ds(k * chunk, chunk), :, m * LANES : (m + 1) * LANES] = (
                ustage[m].reshape(chunk, tile, LANES).astype(BF16)
            )

        def give_back(p):
            return pltpu.make_async_remote_copy(
                src_ref=ret_send.at[p],
                dst_ref=ret_recv.at[me],
                send_sem=send_sems.at[4],
                recv_sem=recv_sems.at[7],
                device_id=(peer_of(p), t),
                device_id_type=MESH,
            )

        for_peers(k, lambda p: give_back(p).start())
        if k == 0:
            ret_recv[me] = ret_send[self_pos]

    get_down.wait()
    for copy in get_ups:
        copy.wait()
    for k in range(CHUNKS):
        arrivals = chunk - 1 if k == 0 else chunk
        wait_bytes(recv.at[pl.ds(0, arrivals)], recv_sems.at[k])
        partial(k)
        total(k)
        corrections(k)

    wait_bytes(bs_recv.at[pl.ds(0, tensors - 1)], recv_sems.at[2])
    base = bs_recv[0].astype(F32)
    for s in range(1, tensors):
        base = base + bs_recv[s].astype(F32)
    k_out[...] = base[:, :LANES].astype(BF16)

    wait_bytes(ret_recv.at[pl.ds(0, holders - 1)], recv_sems.at[7])
    for m in range(MOST + 1):
        stage[m] = (
            ret_recv[:, :, m * LANES : (m + 1) * LANES].astype(F32).reshape(holders * tile, LANES)
        )

    def picked_rows(refs):
        gathered = jnp.concatenate(
            [stage[m, pl.ds(start, adapters, stride=blocks), :] for m, start in refs], axis=0
        ).astype(BF16)
        return jnp.dot(fsel[...], gathered, preferred_element_type=F32)

    for j in range(blocks):
        q_out[:, j * LANES : (j + 1) * LANES] = picked_rows([(m, j) for m in range(MOST)]).astype(
            BF16
        )
    v_out[...] = (base[:, LANES:] + picked_rows([(MOST, m) for m in range(MOST)])).astype(BF16)

    wait_bytes(send.at[pl.ds(0, holders - 1)], send_sems.at[0])
    wait_bytes(bs_send.at[pl.ds(0, tensors - 1)], send_sems.at[1])
    for k in range(CHUNKS):
        wait_bytes(part.at[k, pl.ds(0, tensors - 1)], send_sems.at[2])
        wait_bytes(sh.at[k, pl.ds(0, tensors - 1)], send_sems.at[3])
    wait_bytes(ret_send.at[pl.ds(0, holders - 1)], send_sems.at[4])


def local(holders, tensors, tokens, index, kv_weight, down, up_query, up_value):
    rows, features = tokens.shape
    head = kv_weight.shape[2] // tensors
    per_holder = down.shape[0]
    blocks = features // LANES
    tile = per_holder * blocks
    chunk = holders // CHUNKS
    share = MOST * per_holder * chunk // tensors
    vmem = pltpu.VMEM
    dma = pltpu.SemaphoreType.DMA
    scratch = [
        vmem(tokens.shape, BF16),
        vmem(index.shape, jnp.int32),
        vmem(kv_weight.shape, BF16),
        vmem((2 * features, kv_weight.shape[2]), BF16),
        vmem((2, rows, 2 * features), BF16),
        vmem(down.shape, BF16),
        vmem((per_holder, 2 * up_query.shape[1], features + LANES), BF16),
        vmem((rows, MOST * holders * per_holder), BF16),
        vmem((MOST + 1, holders * tile, LANES), F32),
        vmem((holders, tile, MOST * LANES), BF16),
        vmem((holders, tile, MOST * LANES), BF16),
        vmem((per_holder, MOST * chunk, features), BF16),
        vmem((CHUNKS, tensors, share, LANES), F32),
        vmem((CHUNKS, tensors, share, LANES), F32),
        vmem((CHUNKS, tensors, -(-share // 16) * 16, LANES), BF16),
        vmem((MOST + 1, chunk * tile, LANES), F32),
        vmem((holders, tile, (MOST + 1) * LANES), BF16),
        vmem((holders, tile, (MOST + 1) * LANES), BF16),
        vmem((tensors, rows, 2 * head), BF16),
        vmem((tensors, rows, 2 * head), BF16),
        dma((4 + 2 * per_holder,)),
        dma((5,)),
        dma((8,)),
    ]
    return pl.pallas_call(
        functools.partial(kernel, holders, tensors),
        out_shape=(
            jax.ShapeDtypeStruct((rows, features), BF16),
            jax.ShapeDtypeStruct((rows, head), BF16),
            jax.ShapeDtypeStruct((rows, head), BF16),
        ),
        in_specs=[pl.BlockSpec(memory_space=pl.ANY)] * 6,
        out_specs=tuple([pl.BlockSpec(memory_space=vmem)] * 3),
        scratch_shapes=scratch,
        compiler_params=pltpu.CompilerParams(
            collective_id=0, has_side_effects=True, vmem_limit_bytes=56 << 20
        ),
        name="adapters",
    )(tokens, index, kv_weight, down, up_query, up_value)


def solution(mesh):
    placed = (
        P("adapter", "tensor"),
        P("adapter", None),
        P("tensor", None, None),
        P("adapter", "tensor", None),
        P("adapter", None, "tensor"),
        P("adapter", None, "tensor"),
    )
    return jax.shard_map(
        functools.partial(local, mesh.shape["adapter"], mesh.shape["tensor"]),
        mesh=mesh,
        in_specs=placed,
        out_specs=(P("adapter", "tensor"), P("adapter", "tensor"), P("adapter", "tensor")),
        check_vma=False,
    )
```

time: 134 us -> 77.1 us (0.58)
  Pallas kernels: 0 us -> 70.4 us
  waiting for transfers between devices: 29.1 us -> 0 us
  blocking collectives: 27.9 us -> 0 us
  starting transfers between devices: 27.7 us -> 0 us
  local copies, waits for them, and re-layouts: 26.3 us -> 5.81 us
  between operations: 14.2 us -> 0.64 us
  matrix products: 5.69 us -> 0 us
  other arithmetic: 2.85 us -> 0 us
    pallas_call x0 -> x1, Pallas kernels: none -> 70.4 us  [local(): pl.pallas_call(functools.partial(kernel, holders, tensors), out_shape=(ja...]
    all_to_all x2 -> x0, waiting for transfers between devices: 29.1 us -> none  [the longest x1 23.1 us: local(): lax.all_to_all(jnp.concatenate([delta_q, delta_v], axis=3).astype(jnp.bfl...]
    psum x1 -> x0, blocking collectives: 27.9 us -> none  [local(): reduced_hidden = lax.psum(partial_value, 'tensor').astype(jnp.bfloat16)]
    all_to_all x2 -> x0, starting transfers between devices: 27.7 us -> none  [the longest x1 14.8 us: local(): lax.all_to_all(outgoing, 'adapter', split_axis=0, concat_axis=0, tiled=True)]
    dot_general x1 -> x0, local copies, waits for them, and re-layouts: 6.44 us -> none  [local(): jnp.dot(tokens, flat_weight, preferred_element_type=jnp.float32)]
    dot_general x4 -> x0, matrix products: 5.69 us -> none  [the longest x1 4.71 us: local(): jnp.dot(tokens, flat_weight, preferred_element_type=jnp.float32)]
    gather x3 -> x0, local copies, waits for them, and re-layouts: 5.16 us -> none  [the longest x2 4.26 us: local(): tokens[source_row]]
    scatter x2 -> x0, local copies, waits for them, and re-layouts: 1.98 us -> none  [the longest x1 1.01 us: local(): filled = jnp.zeros((slots_all,), jnp.bool_).at[slot_of].set(True)]
  transfers between devices with their start and end apart: 3 -> 0, of which waited for: 2 -> 0; matrix products, arithmetic and copies ran while one was open for 16% -> 0% of each run, Pallas kernels for 0% -> 0%
where the time goes in v1:
time: 77.1 us; the launch traced here: 76.8 us
  Pallas kernels  70.4 us (91%)
  local copies, waits for them, and re-layouts  5.81 us (8%)
    pallas_call x1, Pallas kernels, local(): pl.pallas_call(functools.partial(kernel, holders, tensors), out_shape=(ja...  70.4 us
    unnamed x4, local copies, waits for them, and re-layouts  5.81 us

profile of v1, /device:TPU:1, one launch (start us, length us, event | category | flops | bytes accessed | tf_op | source)
XLA Modules:
  0.0 76.8 jit_solution(159386798047559598)
XLA Ops:
  0.6 1.4 %copy.9.idx_hbm = s32[128,1]{1,0:T(8,128)} copy(s32[128,1]{0,1:T(1,128)} %param.7) | data formatting | bytes 1024 | tf_op args[1]
  2.0 70.4 %adapters.1 = (bf16[128,1024]{1,0:T(8,128)(2,1)}, bf16[128,128]{1,0:T(8,128)(2,1)}, bf16[128,128]{1,0:T(8,128)(2,1)}) custom-call(bf16[128,1024]{1,0:T(8,128)(2,1)} %tok_hbm.1, s32[128,1]{1,0:T(8,128)} %copy.9.idx_hbm, bf16[1024,2,1024]{2,1,0:T(2,128)(2,1)} %kvw_hbm.1, bf16[2,1024,128]{2,1,0:T(8,128)(2,1)} %down_hbm.1, bf16[2,64,1024]{2,1,0:T(8,128)(2,1)} %upq_hbm.1, ...), custom_call_target="tpu_custom_call" | custom-call | tf_op jit(solution)/shard_map/adapters/pallas_call | solution.py:376
  72.4 1.7 %copy.13 = bf16[128,1024]{1,0:T(8,128)(2,1)} copy(bf16[128,1024]{1,0:T(8,128)(2,1)} %get-tuple-element.6) | data formatting | bytes 524288
  74.1 1.4 %copy.14 = bf16[128,128]{1,0:T(8,128)(2,1)} copy(bf16[128,128]{1,0:T(8,128)(2,1)} %get-tuple-element.7) | data formatting | bytes 65536
  75.5 1.4 %copy.15 = bf16[128,128]{1,0:T(8,128)(2,1)} copy(bf16[128,128]{1,0:T(8,128)(2,1)} %get-tuple-element.8) | data formatting | bytes 65536

commit v2 on v1

v2 whole, which is shorter than its diff:
```python
import functools
import jax
import jax.numpy as jnp
from jax import lax
from jax.experimental import pallas as pl
from jax.experimental.pallas import tpu as pltpu
from jax.sharding import PartitionSpec as P

MESH = pl.DeviceIdType.MESH
LANES = 128
BF16 = jnp.bfloat16
F32 = jnp.float32
MOST = 3
ZS, XS, CORES = 8, 4, 2
CHUNKS = 4


def kernel(
    holders,
    tensors,
    tok_hbm,
    idx_hbm,
    kvw_hbm,
    down_hbm,
    upq_hbm,
    upv_hbm,
    q_out,
    k_out,
    v_out,
    tok,
    idx,
    kvw,
    wbase,
    lhs,
    down,
    up,
    fsel,
    stage,
    send,
    recv,
    xs,
    part,
    rs,
    sh,
    ustage,
    ret_send,
    ret_recv,
    bs_send,
    bs_recv,
    load_sems,
    send_sems,
    recv_sems,
):
    me = lax.axis_index("adapter")
    t = lax.axis_index("tensor")
    rows, features = tok.shape
    blocks = features // LANES
    per_holder = down.shape[0]
    adapters = holders * per_holder
    tile = per_holder * blocks
    chunk = holders // CHUNKS
    z = me // (XS * CORES)
    x = (me // CORES) % XS
    core = me % CORES
    self_pos = z * CORES + core

    def peer_of(p):
        offset = p // chunk
        px = (x + offset % 2 * (1 - 2 * (x % 2)) + 2 * (offset // 2)) % XS
        return ((p // CORES) % ZS) * (XS * CORES) + px * CORES + p % CORES

    def my_pos(p):
        return (p // chunk) * chunk + self_pos

    def position(k, d):
        return k * chunk + (self_pos + d) % chunk

    def for_peers(k, act):
        @pl.loop(1 if k == 0 else 0, chunk)
        def _(d):
            act(position(k, d))

    get_tok = pltpu.make_async_copy(tok_hbm, tok, load_sems.at[0])
    get_idx = pltpu.make_async_copy(idx_hbm, idx, load_sems.at[1])
    get_kvw = pltpu.make_async_copy(kvw_hbm, kvw, load_sems.at[2])
    get_down = pltpu.make_async_copy(down_hbm, down, load_sems.at[3])
    get_idx.start()
    get_tok.start()

    barrier = pltpu.get_barrier_semaphore()

    @pl.loop(1, tensors)
    def _(d):
        pl.semaphore_signal(barrier, inc=1, device_id=(me, (t + d) % tensors), device_id_type=MESH)

    @pl.loop(1, holders)
    def _(d):
        pl.semaphore_signal(barrier, inc=1, device_id=((me + d) % holders, t), device_id_type=MESH)

    get_down.start()
    get_kvw.start()

    get_idx.wait()
    picked = (lax.broadcasted_iota(jnp.int32, (adapters, rows), 0) == idx[...]).astype(F32)
    earlier = lax.broadcasted_iota(jnp.int32, (rows, rows), 0) < lax.broadcasted_iota(
        jnp.int32, (rows, rows), 1
    )
    ordinal = jnp.dot(
        picked.astype(BF16), earlier.astype(F32).astype(BF16), preferred_element_type=F32
    )
    get_tok.wait()
    for m in range(MOST):
        chosen = jnp.where(ordinal == float(m), picked, 0.0)
        fsel[m * adapters : (m + 1) * adapters, :] = chosen
        gathered = jnp.dot(chosen.astype(BF16), tok[...], preferred_element_type=F32)
        for j in range(blocks):
            stage[m, pl.ds(j, adapters, stride=blocks), :] = gathered[:, j * LANES : (j + 1) * LANES]
        send[:, :, m * LANES : (m + 1) * LANES] = (
            stage[m].reshape(holders, tile, LANES).astype(BF16)
        )

    pl.semaphore_wait(barrier, tensors - 1 + holders - 1)

    def dispatch(k, p):
        return pltpu.make_async_remote_copy(
            src_ref=send.at[peer_of(p)],
            dst_ref=recv.at[my_pos(p)],
            send_sem=send_sems.at[0],
            recv_sem=recv_sems.at[3 + 2 * CHUNKS + k],
            device_id=(peer_of(p), t),
            device_id_type=MESH,
        )

    def dispatch_chunk(k):
        for_peers(k, lambda p: dispatch(k, p).start())

    dispatch_chunk(0)
    dispatch_chunk(1)
    recv[self_pos] = send[me]

    up[...] = jnp.zeros_like(up)
    get_ups = []
    for a in range(per_holder):
        rank = upq_hbm.shape[1]
        get_ups.append(
            pltpu.make_async_copy(
                upq_hbm.at[a], up.at[a, pl.ds(0, rank), pl.ds(0, features)], load_sems.at[4 + a]
            )
        )
        get_ups.append(
            pltpu.make_async_copy(
                upv_hbm.at[a],
                up.at[a, pl.ds(rank, rank), pl.ds(features, LANES)],
                load_sems.at[4 + per_holder + a],
            )
        )
    for copy in get_ups:
        copy.start()
    for c in range(2):
        spread = (
            lax.broadcasted_iota(jnp.int32, (LANES, 2 * LANES), 1)
            == 2 * lax.broadcasted_iota(jnp.int32, (LANES, 2 * LANES), 0) + c
        ).astype(F32).astype(BF16)
        for j in range(blocks):
            lhs[c, :, 2 * j * LANES : 2 * (j + 1) * LANES] = jnp.dot(
                tok[:, j * LANES : (j + 1) * LANES], spread, preferred_element_type=F32
            ).astype(BF16)
    dispatch_chunk(2)
    get_kvw.wait()
    run = 32

    @pl.loop(0, features // run)
    def _(i):
        wbase[pl.ds(i * 2 * run, 2 * run), :] = kvw[pl.ds(i * run, run)].reshape(
            2 * run, wbase.shape[1]
        )

    @pl.loop(0, tensors // 2)
    def _(n):
        columns = pl.ds(pl.multiple_of(n * 2 * LANES, 2 * LANES), 2 * LANES)
        for c in range(2):
            terms = jnp.dot(lhs[c], wbase[:, columns], preferred_element_type=F32).astype(BF16)
            for half in range(2):
                bs_send[2 * n + half, :, c * LANES : (c + 1) * LANES] = terms[
                    :, half * LANES : (half + 1) * LANES
                ]

    dispatch_chunk(3)
    def base_copy(d):
        other = (t + d) % tensors
        return pltpu.make_async_remote_copy(
            src_ref=bs_send.at[other],
            dst_ref=bs_recv.at[t],
            send_sem=send_sems.at[1],
            recv_sem=recv_sems.at[2],
            device_id=(me, other),
            device_id_type=MESH,
        )

    bs_recv[t] = bs_send[t]
    ustage[MOST] = jnp.zeros_like(ustage[MOST])

    owners = MOST * per_holder

    def wait_bytes(ref, sem):
        pltpu.make_async_copy(ref, ref, sem).wait()

    def partial(k):
        for m in range(MOST):
            stage[m, pl.ds(0, chunk * tile), :] = (
                recv[pl.ds(k * chunk, chunk), :, m * LANES : (m + 1) * LANES]
                .astype(F32)
                .reshape(chunk * tile, LANES)
            )
        for a in range(per_holder):
            for m in range(MOST):
                for j in range(blocks):
                    xs[a, m * chunk : (m + 1) * chunk, j * LANES : (j + 1) * LANES] = stage[
                        m, pl.ds(a * blocks + j, chunk, stride=tile), :
                    ].astype(BF16)
            terms = jnp.dot(xs[a], down[a], preferred_element_type=F32)
            for m in range(MOST):
                part[k, a * MOST + m] = terms[m * chunk : (m + 1) * chunk]

        @pl.loop(1, tensors)
        def _(d):
            other = (t + d) % tensors

            @pl.when(other < owners)
            def _():
                pltpu.make_async_remote_copy(
                    src_ref=part.at[k, other],
                    dst_ref=rs.at[k, t],
                    send_sem=send_sems.at[2],
                    recv_sem=recv_sems.at[3 + k],
                    device_id=(me, other),
                    device_id_type=MESH,
                ).start()

    def total(k):
        @pl.when(t < owners)
        def _():
            rs[k, t] = part[k, t]
            wait_bytes(rs.at[k, pl.ds(0, tensors - 1)], recv_sems.at[3 + k])
            summed = rs[k, 0]
            for s in range(1, tensors):
                summed = summed + rs[k, s]
            sh[k, t] = summed.astype(BF16)

            @pl.loop(1, tensors)
            def _(d):
                pltpu.make_async_remote_copy(
                    src_ref=sh.at[k, t],
                    dst_ref=sh.at[k, t],
                    send_sem=send_sems.at[3],
                    recv_sem=recv_sems.at[3 + CHUNKS + k],
                    device_id=(me, (t + d) % tensors),
                    device_id_type=MESH,
                ).start()

    def corrections(k):
        @pl.when(t < owners)
        def _():
            wait_bytes(sh.at[k, pl.ds(0, owners - 1)], recv_sems.at[3 + CHUNKS + k])

        @pl.when(t >= owners)
        def _():
            wait_bytes(sh.at[k, pl.ds(0, owners)], recv_sems.at[3 + CHUNKS + k])

        for a in range(per_holder):
            shrunk = sh[k, a * MOST : (a + 1) * MOST].reshape(MOST * chunk, LANES)
            deltas = jnp.dot(shrunk, up[a], preferred_element_type=F32)
            for m in range(MOST):
                of_m = deltas[m * chunk : (m + 1) * chunk]
                for j in range(blocks):
                    ustage[m, pl.ds(a * blocks + j, chunk, stride=tile), :] = of_m[
                        :, j * LANES : (j + 1) * LANES
                    ]
                ustage[MOST, pl.ds(a * blocks + m, chunk, stride=tile), :] = of_m[:, features:]
        for m in range(MOST + 1):
            ret_send[pl.ds(k * chunk, chunk), :, m * LANES : (m + 1) * LANES] = (
                ustage[m].reshape(chunk, tile, LANES).astype(BF16)
            )

        def give_back(p):
            return pltpu.make_async_remote_copy(
                src_ref=ret_send.at[p],
                dst_ref=ret_recv.at[me],
                send_sem=send_sems.at[4],
                recv_sem=recv_sems.at[0],
                device_id=(peer_of(p), t),
                device_id_type=MESH,
            )

        for_peers(k, lambda p: give_back(p).start())
        if k == 0:
            ret_recv[me] = ret_send[self_pos]

    def arrive(k):
        arrivals = chunk - 1 if k == 0 else chunk
        wait_bytes(recv.at[pl.ds(0, arrivals)], recv_sems.at[3 + 2 * CHUNKS + k])
        partial(k)

    def base_sends():
        @pl.loop(1, tensors)
        def _(d):
            base_copy(d).start()

    get_down.wait()
    for copy in get_ups:
        copy.wait()
    steps = ("a0", "a1", "b0", "a2", "b1", "c0", "a3", "b2", "c1", "b3", "base", "c2", "c3")
    for name in steps:
        if name == "base":
            base_sends()
        elif name[0] == "a":
            arrive(int(name[1]))
        elif name[0] == "b":
            total(int(name[1]))
        else:
            corrections(int(name[1]))

    wait_bytes(bs_recv.at[pl.ds(0, tensors - 1)], recv_sems.at[2])
    base = bs_recv[0].astype(F32)
    for s in range(1, tensors):
        base = base + bs_recv[s].astype(F32)
    k_out[...] = base[:, :LANES].astype(BF16)

    wait_bytes(ret_recv.at[pl.ds(0, holders - 1)], recv_sems.at[0])
    for m in range(MOST + 1):
        stage[m] = (
            ret_recv[:, :, m * LANES : (m + 1) * LANES].astype(F32).reshape(holders * tile, LANES)
        )

    chosen_rows = fsel[...].T.astype(BF16)

    def picked_rows(refs):
        gathered = jnp.concatenate(
            [stage[m, pl.ds(start, adapters, stride=blocks), :] for m, start in refs], axis=0
        ).astype(BF16)
        return jnp.dot(chosen_rows, gathered, preferred_element_type=F32)

    for j in range(blocks):
        q_out[:, j * LANES : (j + 1) * LANES] = picked_rows([(m, j) for m in range(MOST)]).astype(
            BF16
        )
    v_out[...] = (base[:, LANES:] + picked_rows([(MOST, m) for m in range(MOST)])).astype(BF16)

    wait_bytes(send.at[pl.ds(0, holders - 1)], send_sems.at[0])
    wait_bytes(bs_send.at[pl.ds(0, tensors - 1)], send_sems.at[1])

    @pl.when(t < owners)
    def _():
        for k in range(CHUNKS):
            wait_bytes(part.at[k, pl.ds(0, owners - 1)], send_sems.at[2])
            wait_bytes(rs.at[k, pl.ds(0, tensors - 1), pl.ds(0, chunk // 2)], send_sems.at[3])

    @pl.when(t >= owners)
    def _():
        for k in range(CHUNKS):
            wait_bytes(part.at[k, pl.ds(0, owners)], send_sems.at[2])

    wait_bytes(ret_send.at[pl.ds(0, holders - 1)], send_sems.at[4])


def step(holders, tensors, tokens, index, kv_weight, down, up_query, up_value):
    rows, features = tokens.shape
    head = kv_weight.shape[2] // tensors
    per_holder = down.shape[0]
    blocks = features // LANES
    tile = per_holder * blocks
    chunk = holders // CHUNKS
    owners = MOST * per_holder
    vmem = pltpu.VMEM
    dma = pltpu.SemaphoreType.DMA
    scratch = [
        vmem(tokens.shape, BF16),
        vmem((1, rows), jnp.int32),
        vmem(kv_weight.shape, BF16),
        vmem((2 * features, kv_weight.shape[2]), BF16),
        vmem((2, rows, 2 * features), BF16),
        vmem(down.shape, BF16),
        vmem((per_holder, 2 * up_query.shape[1], features + LANES), BF16),
        vmem((MOST * holders * per_holder, rows), F32),
        vmem((MOST + 1, holders * tile, LANES), F32),
        vmem((holders, tile, MOST * LANES), BF16),
        vmem((holders, tile, MOST * LANES), BF16),
        vmem((per_holder, MOST * chunk, features), BF16),
        vmem((CHUNKS, owners, chunk, LANES), F32),
        vmem((CHUNKS, tensors, chunk, LANES), F32),
        vmem((CHUNKS, owners, chunk, LANES), BF16),
        vmem((MOST + 1, chunk * tile, LANES), F32),
        vmem((holders, tile, (MOST + 1) * LANES), BF16),
        vmem((holders, tile, (MOST + 1) * LANES), BF16),
        vmem((tensors, rows, 2 * head), BF16),
        vmem((tensors, rows, 2 * head), BF16),
        dma((4 + 2 * per_holder,)),
        dma((5,)),
        dma((3 + 3 * CHUNKS,)),
    ]
    return pl.pallas_call(
        functools.partial(kernel, holders, tensors),
        out_shape=(
            jax.ShapeDtypeStruct((rows, features), BF16),
            jax.ShapeDtypeStruct((rows, head), BF16),
            jax.ShapeDtypeStruct((rows, head), BF16),
        ),
        in_specs=[pl.BlockSpec(memory_space=pl.ANY)] * 6,
        out_specs=tuple([pl.BlockSpec(memory_space=vmem)] * 3),
        scratch_shapes=scratch,
        compiler_params=pltpu.CompilerParams(
            collective_id=0, has_side_effects=True, vmem_limit_bytes=56 << 20
        ),
        name="adapters",
    )(tokens, index.reshape(1, rows), kv_weight, down, up_query, up_value)


def hand_over(*refs):
    count = len(refs) // 2
    for i in range(count):
        refs[count + i][...] = refs[i][...]


def local(holders, tensors, *operands):
    outs = step(holders, tensors, *operands)
    whole = [pl.BlockSpec(memory_space=pltpu.VMEM)] * len(outs)
    return pl.pallas_call(
        hand_over,
        out_shape=tuple(jax.ShapeDtypeStruct(o.shape, o.dtype) for o in outs),
        in_specs=whole,
        out_specs=tuple(whole),
        name="hand_over",
    )(*outs)


def solution(mesh):
    placed = (
        P("adapter", "tensor"),
        P("adapter", None),
        P("tensor", None, None),
        P("adapter", "tensor", None),
        P("adapter", None, "tensor"),
        P("adapter", None, "tensor"),
    )
    return jax.shard_map(
        functools.partial(local, mesh.shape["adapter"], mesh.shape["tensor"]),
        mesh=mesh,
        in_specs=placed,
        out_specs=(P("adapter", "tensor"), P("adapter", "tensor"), P("adapter", "tensor")),
        check_vma=False,
    )
```

time: 77.1 us -> 65.7 us (0.85)
  local copies, waits for them, and re-layouts: 5.81 us -> 0 us
  Pallas kernels: 70.4 us -> 64.9 us
    unnamed x4 -> x0, local copies, waits for them, and re-layouts: 5.81 us -> none
    pallas_call x1 -> x2, Pallas kernels: 70.4 us -> 64.9 us  [the longest x1 63.2 us: step(): pl.pallas_call(functools.partial(kernel, holders, tensors), out_shape=(ja...]
where the time goes in v2:
time: 65.7 us; the launch traced here: 65.5 us
  Pallas kernels  64.9 us (99%)
    pallas_call x1, Pallas kernels, step(): pl.pallas_call(functools.partial(kernel, holders, tensors), out_shape=(ja...  63.2 us
    pallas_call x1, Pallas kernels, local(): pl.pallas_call(hand_over, out_shape=tuple((jax.ShapeDtypeStruct(o.shape,...  1.7 us

profile of v2, /device:TPU:1, one launch (start us, length us, event | category | flops | bytes accessed | tf_op | source)
XLA Modules:
  0.0 65.5 jit_solution(4973158442340582866)
XLA Ops:
  0.6 63.2 %adapters.1 = (bf16[128,1024]{1,0:T(8,128)(2,1)}, bf16[128,128]{1,0:T(8,128)(2,1)}, bf16[128,128]{1,0:T(8,128)(2,1)}) custom-call(bf16[128,1024]{1,0:T(8,128)(2,1)} %tok_hbm.1, s32[1,128]{1,0:T(1,128)} %bitcast.1, bf16[1024,2,1024]{2,1,0:T(2,128)(2,1)} %kvw_hbm.1, bf16[2,1024,128]{2,1,0:T(8,128)(2,1)} %down_hbm.1, bf16[2,64,1024]{2,1,0:T(8,128)(2,1)} %upq_hbm.1, ...), custom_call_target="tpu_custom_call" | custom-call | tf_op jit(solution)/shard_map/adapters/pallas_call | solution.py:401
  63.8 1.7 %hand_over.1 = (bf16[128,1024]{1,0:T(8,128)(2,1)}, bf16[128,128]{1,0:T(8,128)(2,1)}, bf16[128,128]{1,0:T(8,128)(2,1)}) custom-call(bf16[128,1024]{1,0:T(8,128)(2,1)} %get-tuple-element.6.refs_0_, bf16[128,128]{1,0:T(8,128)(2,1)} %get-tuple-element.7.refs_1_, bf16[128,128]{1,0:T(8,128)(2,1)} %get-tuple-element.8.refs_2_), custom_call_target="tpu_custom_call" | custom-call | tf_op jit(solution)/shard_map/hand_over/pallas_call | solution.py:427

commit v3 on v2

v3 whole, which is shorter than its diff:
```python
import functools
import jax
import jax.numpy as jnp
from jax import lax
from jax.experimental import pallas as pl
from jax.experimental.pallas import tpu as pltpu
from jax.sharding import PartitionSpec as P

MESH = pl.DeviceIdType.MESH
LANES = 128
BF16 = jnp.bfloat16
F32 = jnp.float32
MOST = 3
ZS, XS, CORES = 8, 4, 2
CHUNKS = XS
STEPS = (
    "a0", "b0", "a1", "c0", "b1", "a2", "a3", "b2", "c1", "b3", "c2", "s1", "v0", "v1", "v2",
    "c3", "v3", "f0", "f1", "f2", "base", "values", "f3",
)
BASE_TO = ((1, 7), (2, 6, 3, 5, 4))
R_BASE, R_V, R_TOK = 0, 1, 2
R_SUM, R_SHRUNK, R_RET, R_PAIR = (R_TOK + i * CHUNKS for i in range(1, 5))
S_TOK, S_BASE, S_SUM, S_SHRUNK, S_RET, S_PAIR, S_V = range(7)


def kernel(
    holders,
    tensors,
    tok_hbm,
    idx_hbm,
    kvw_hbm,
    down_hbm,
    upq_hbm,
    upv_hbm,
    q_out,
    k_out,
    v_out,
    tok,
    idx,
    kvw,
    wbase,
    lhs,
    down,
    up,
    fsel,
    fturn,
    vsel,
    stage,
    send,
    recv,
    xs,
    part,
    rs,
    sh,
    ustage,
    ret_send,
    ret_recv,
    ys,
    q_sum,
    v_all,
    v_pair,
    v_send,
    v_recv,
    bs_send,
    bs_recv,
    load_sems,
    send_sems,
    recv_sems,
):
    me = lax.axis_index("adapter")
    t = lax.axis_index("tensor")
    rows, features = tok.shape
    blocks = features // LANES
    per_holder = down.shape[0]
    adapters = holders * per_holder
    tile = per_holder * blocks
    chunk = holders // CHUNKS
    chunk_adapters = chunk * per_holder
    owners = MOST * per_holder
    z = me // (XS * CORES)
    x = (me // CORES) % XS
    core = me % CORES
    sibling = me + 1 - 2 * core
    self_pos = z * CORES + core

    def peer_of(p):
        offset = p // chunk
        px = (x + offset % 2 * (1 - 2 * (x % 2)) + 2 * (offset // 2)) % XS
        return ((p // CORES) % ZS) * (XS * CORES) + px * CORES + p % CORES

    def my_pos(p):
        return (p // chunk) * chunk + self_pos

    def for_peers(k, act):
        @pl.loop(1 if k == 0 else 0, chunk)
        def _(d):
            act(k * chunk + (self_pos + d) % chunk)

    def wait_bytes(ref, sem):
        pltpu.make_async_copy(ref, ref, sem).wait()

    def remote(src, dst, send_sem, recv_sem, device):
        return pltpu.make_async_remote_copy(
            src_ref=src,
            dst_ref=dst,
            send_sem=send_sems.at[send_sem],
            recv_sem=recv_sems.at[recv_sem],
            device_id=device,
            device_id_type=MESH,
        )

    get_tok = pltpu.make_async_copy(tok_hbm, tok, load_sems.at[0])
    get_idx = pltpu.make_async_copy(idx_hbm, idx, load_sems.at[1])
    get_kvw = pltpu.make_async_copy(kvw_hbm, kvw, load_sems.at[2])
    get_down = pltpu.make_async_copy(down_hbm, down, load_sems.at[3])
    get_idx.start()
    get_tok.start()

    barrier = pltpu.get_barrier_semaphore()

    @pl.loop(1, tensors, unroll=7)
    def _(d):
        pl.semaphore_signal(barrier, inc=1, device_id=(me, (t + d) % tensors), device_id_type=MESH)

    @pl.loop(1, holders, unroll=holders - 1)
    def _(d):
        pl.semaphore_signal(barrier, inc=1, device_id=((me + d) % holders, t), device_id_type=MESH)

    get_down.start()
    get_kvw.start()

    get_idx.wait()
    ids = idx[...]
    px = (ids >> 2) & 3
    offset = ((x + px) & 1) + 2 * (((x // 2) + (px >> 1)) & 1)
    place = offset * chunk_adapters + (ids >> 4) * (CORES * per_holder) + (ids & 3)
    places = lax.broadcasted_iota(jnp.int32, (adapters, rows), 0)
    picked = (places == place).astype(F32)
    earlier = lax.broadcasted_iota(jnp.int32, (rows, rows), 0) < lax.broadcasted_iota(
        jnp.int32, (rows, rows), 1
    )
    ordinal = jnp.dot(
        picked.astype(BF16), earlier.astype(F32).astype(BF16), preferred_element_type=F32
    )
    get_tok.wait()
    for m in range(MOST):
        chosen = jnp.where(ordinal == float(m), picked, 0.0)
        fsel[:, m * chunk_adapters : (m + 1) * chunk_adapters, :] = chosen.reshape(
            CHUNKS, chunk_adapters, rows
        )
        gathered = jnp.dot(chosen.astype(BF16), tok[...], preferred_element_type=F32)
        for j in range(blocks):
            stage[m, pl.ds(j, adapters, stride=blocks), :] = gathered[:, j * LANES : (j + 1) * LANES]
        send[:, :, m * LANES : (m + 1) * LANES] = (
            stage[m].reshape(holders, tile, LANES).astype(BF16)
        )

    pl.semaphore_wait(barrier, tensors - 1 + holders - 1)

    def dispatch_chunk(k):
        for_peers(
            k,
            lambda p: remote(
                send.at[p], recv.at[my_pos(p)], S_TOK, R_TOK + k, (peer_of(p), t)
            ).start(),
        )

    dispatch_chunk(0)
    recv[self_pos] = send[self_pos]

    up[...] = jnp.zeros_like(up)
    get_ups = []
    for a in range(per_holder):
        rank = upq_hbm.shape[1]
        get_ups.append(
            pltpu.make_async_copy(
                upq_hbm.at[a], up.at[a, pl.ds(0, rank), pl.ds(0, features)], load_sems.at[4 + a]
            )
        )
        get_ups.append(
            pltpu.make_async_copy(
                upv_hbm.at[a],
                up.at[a, pl.ds(rank, rank), pl.ds(features, LANES)],
                load_sems.at[4 + per_holder + a],
            )
        )
    for copy in get_ups:
        copy.start()
    for c in range(2):
        spread = (
            lax.broadcasted_iota(jnp.int32, (LANES, 2 * LANES), 1)
            == 2 * lax.broadcasted_iota(jnp.int32, (LANES, 2 * LANES), 0) + c
        ).astype(F32).astype(BF16)
        for j in range(blocks):
            lhs[c, :, 2 * j * LANES : 2 * (j + 1) * LANES] = jnp.dot(
                tok[:, j * LANES : (j + 1) * LANES], spread, preferred_element_type=F32
            ).astype(BF16)
    dispatch_chunk(1)
    get_kvw.wait()
    run = 32

    @pl.loop(0, features // run)
    def _(i):
        wbase[pl.ds(i * 2 * run, 2 * run), :] = kvw[pl.ds(i * run, run)].reshape(
            2 * run, wbase.shape[1]
        )

    dispatch_chunk(2)
    @pl.loop(0, tensors // 2)
    def _(n):
        columns = pl.ds(pl.multiple_of(n * 2 * LANES, 2 * LANES), 2 * LANES)
        for c in range(2):
            terms = jnp.dot(lhs[c], wbase[:, columns], preferred_element_type=F32).astype(BF16)
            for half in range(2):
                bs_send[2 * n + half, :, c * LANES : (c + 1) * LANES] = terms[
                    :, half * LANES : (half + 1) * LANES
                ]

    dispatch_chunk(3)

    def base_sends(ds):
        for d in ds:
            other = (t + d) % tensors
            remote(bs_send.at[other], bs_recv.at[t], S_BASE, R_BASE, (me, other)).start()

    base_sends(BASE_TO[0])
    bs_recv[t] = bs_send[t]
    ustage[MOST] = jnp.zeros_like(ustage[MOST])
    for k in range(CHUNKS):
        fturn[k] = fsel[k].T.astype(BF16)
    pairs = adapters // (CORES * per_holder)
    turned = (places == (place & 3) * pairs + (place >> 2)).astype(F32)
    turned_ordinal = jnp.dot(
        turned.astype(BF16), earlier.astype(F32).astype(BF16), preferred_element_type=F32
    )
    for m in range(MOST):
        chosen = jnp.where(turned_ordinal == float(m), turned, 0.0)
        vsel[:, m * adapters : (m + 1) * adapters] = chosen.T.astype(BF16)
    get_down.wait()
    for copy in get_ups:
        copy.wait()

    def arrive(k):
        wait_bytes(recv.at[pl.ds(0, chunk - 1 if k == 0 else chunk)], recv_sems.at[R_TOK + k])
        for m in range(MOST):
            stage[m, pl.ds(0, chunk * tile), :] = (
                recv[pl.ds(k * chunk, chunk), :, m * LANES : (m + 1) * LANES]
                .astype(F32)
                .reshape(chunk * tile, LANES)
            )
        for a in range(per_holder):
            for m in range(MOST):
                for j in range(blocks):
                    xs[a, m * chunk : (m + 1) * chunk, j * LANES : (j + 1) * LANES] = stage[
                        m, pl.ds(a * blocks + j, chunk, stride=tile), :
                    ].astype(BF16)
            terms = jnp.dot(xs[a], down[a], preferred_element_type=F32)
            for m in range(MOST):
                part[k, a * MOST + m] = terms[m * chunk : (m + 1) * chunk]

        @pl.loop(1, tensors)
        def _(d):
            other = (t + d) % tensors

            @pl.when(other < owners)
            def _():
                remote(part.at[k, other], rs.at[k, t], S_SUM, R_SUM + k, (me, other)).start()

    def total(k):
        @pl.when(t < owners)
        def _():
            rs[k, t] = part[k, t]
            wait_bytes(rs.at[k, pl.ds(0, tensors - 1)], recv_sems.at[R_SUM + k])
            summed = rs[k, 0]
            for s in range(1, tensors):
                summed = summed + rs[k, s]
            sh[k, t] = summed.astype(BF16)

            @pl.loop(1, tensors)
            def _(d):
                other = (t + d) % tensors
                remote(sh.at[k, t], sh.at[k, t], S_SHRUNK, R_SHRUNK + k, (me, other)).start()

    def corrections(k):
        @pl.when(t < owners)
        def _():
            wait_bytes(sh.at[k, pl.ds(0, owners - 1)], recv_sems.at[R_SHRUNK + k])

        @pl.when(t >= owners)
        def _():
            wait_bytes(sh.at[k, pl.ds(0, owners)], recv_sems.at[R_SHRUNK + k])

        for a in range(per_holder):
            shrunk = sh[k, a * MOST : (a + 1) * MOST].reshape(MOST * chunk, LANES)
            deltas = jnp.dot(shrunk, up[a], preferred_element_type=F32)
            for m in range(MOST):
                of_m = deltas[m * chunk : (m + 1) * chunk]
                for j in range(blocks):
                    ustage[m, pl.ds(a * blocks + j, chunk, stride=tile), :] = of_m[
                        :, j * LANES : (j + 1) * LANES
                    ]
                ustage[
                    MOST, pl.ds(a * blocks + m + core * (blocks // 2), chunk, stride=tile), :
                ] = of_m[:, features:]
        v_all[k] = ustage[MOST].reshape(ZS, CORES, tile, LANES).astype(BF16)
        remote(
            v_all.at[k, :, 1 - core], v_pair.at[k], S_PAIR, R_PAIR + k, (sibling, t)
        ).start()
        for m in range(MOST):
            ret_send[pl.ds(k * chunk, chunk), :, m * LANES : (m + 1) * LANES] = (
                ustage[m].reshape(chunk, tile, LANES).astype(BF16)
            )
        for_peers(
            k,
            lambda p: remote(
                ret_send.at[p], ret_recv.at[my_pos(p)], S_RET, R_RET + k, (peer_of(p), t)
            ).start(),
        )
        if k == 0:
            ret_recv[self_pos] = ret_send[self_pos]

    def value_tiles(k):
        wait_bytes(v_pair.at[k], recv_sems.at[R_PAIR + k])
        v_send[k] = v_all[k, :, core] + v_pair[k]

        @pl.loop(1 if k == 0 else 0, ZS)
        def _(d):
            to = (z + d) % ZS
            p = k * chunk + to * CORES + core
            remote(v_send.at[k, to], v_recv.at[k * ZS + z], S_V, R_V, (peer_of(p), t)).start()

        if k == 0:
            v_recv[z] = v_send[k, z]

    def base_sum():
        wait_bytes(bs_recv.at[pl.ds(0, tensors - 1)], recv_sems.at[R_BASE])
        base = bs_recv[0].astype(F32)
        for s in range(1, tensors):
            base = base + bs_recv[s].astype(F32)
        k_out[...] = base[:, :LANES].astype(BF16)
        return base[:, LANES:]

    def select_back(k):
        wait_bytes(
            ret_recv.at[pl.ds(0, chunk - 1 if k == 0 else chunk)], recv_sems.at[R_RET + k]
        )
        for m in range(MOST):
            stage[m, pl.ds(0, chunk * tile), :] = (
                ret_recv[pl.ds(k * chunk, chunk), :, m * LANES : (m + 1) * LANES]
                .astype(F32)
                .reshape(chunk * tile, LANES)
            )
            for j in range(blocks):
                ys[
                    m * chunk_adapters : (m + 1) * chunk_adapters, j * LANES : (j + 1) * LANES
                ] = stage[m, pl.ds(j, chunk_adapters, stride=blocks), :].astype(BF16)
        found = jnp.dot(fturn[k], ys[...], preferred_element_type=F32)
        if k == 0:
            q_sum[...] = found
        elif k < CHUNKS - 1:
            q_sum[...] += found
        else:
            q_out[...] = (q_sum[...] + found).astype(BF16)

    def add_values(base_values):
        wait_bytes(v_recv.at[pl.ds(0, pairs - 1)], recv_sems.at[R_V])
        stage[0, pl.ds(0, pairs * tile), :] = v_recv[...].astype(F32).reshape(pairs * tile, LANES)
        gathered = jnp.concatenate(
            [
                stage[0, pl.ds(a * blocks + c * (blocks // 2) + m, pairs, stride=tile), :]
                for m in range(MOST)
                for c in range(CORES)
                for a in range(per_holder)
            ],
            axis=0,
        ).astype(BF16)
        v_out[...] = (
            base_values + jnp.dot(vsel[...], gathered, preferred_element_type=F32)
        ).astype(BF16)

    base_values = None
    for name in STEPS:
        if name == "base":
            base_values = base_sum()
        elif name == "values":
            add_values(base_values)
        else:
            of = {
                "a": arrive,
                "b": total,
                "c": corrections,
                "v": value_tiles,
                "f": select_back,
                "s": lambda k: base_sends(BASE_TO[k]),
            }
            of[name[0]](int(name[1]))

    wait_bytes(send.at[pl.ds(0, holders - 1)], send_sems.at[S_TOK])
    wait_bytes(bs_send.at[pl.ds(0, tensors - 1)], send_sems.at[S_BASE])

    @pl.when(t < owners)
    def _():
        for k in range(CHUNKS):
            wait_bytes(part.at[k, pl.ds(0, owners - 1)], send_sems.at[S_SUM])
            wait_bytes(
                rs.at[k, pl.ds(0, tensors - 1), pl.ds(0, chunk // 2)], send_sems.at[S_SHRUNK]
            )

    @pl.when(t >= owners)
    def _():
        for k in range(CHUNKS):
            wait_bytes(part.at[k, pl.ds(0, owners)], send_sems.at[S_SUM])

    wait_bytes(ret_send.at[pl.ds(0, holders - 1)], send_sems.at[S_RET])
    wait_bytes(v_pair, send_sems.at[S_PAIR])
    wait_bytes(v_recv.at[pl.ds(0, pairs - 1)], send_sems.at[S_V])


def step(holders, tensors, tokens, index, kv_weight, down, up_query, up_value):
    rows, features = tokens.shape
    head = kv_weight.shape[2] // tensors
    per_holder = down.shape[0]
    blocks = features // LANES
    tile = per_holder * blocks
    chunk = holders // CHUNKS
    owners = MOST * per_holder
    adapters = holders * per_holder
    pairs = holders // CORES
    vmem = pltpu.VMEM
    dma = pltpu.SemaphoreType.DMA
    scratch = [
        vmem(tokens.shape, BF16),
        vmem((1, rows), jnp.int32),
        vmem(kv_weight.shape, BF16),
        vmem((2 * features, kv_weight.shape[2]), BF16),
        vmem((2, rows, 2 * features), BF16),
        vmem(down.shape, BF16),
        vmem((per_holder, 2 * up_query.shape[1], features + LANES), BF16),
        vmem((CHUNKS, MOST * chunk * per_holder, rows), F32),
        vmem((CHUNKS, rows, MOST * chunk * per_holder), BF16),
        vmem((rows, MOST * adapters), BF16),
        vmem((MOST, holders * tile, LANES), F32),
        vmem((holders, tile, MOST * LANES), BF16),
        vmem((holders, tile, MOST * LANES), BF16),
        vmem((per_holder, MOST * chunk, features), BF16),
        vmem((CHUNKS, owners, chunk, LANES), F32),
        vmem((CHUNKS, tensors, chunk, LANES), F32),
        vmem((CHUNKS, owners, chunk, LANES), BF16),
        vmem((MOST + 1, chunk * tile, LANES), F32),
        vmem((holders, tile, MOST * LANES), BF16),
        vmem((holders, tile, MOST * LANES), BF16),
        vmem((MOST * chunk * per_holder, features), BF16),
        vmem((rows, features), F32),
        vmem((CHUNKS, ZS, CORES, tile, LANES), BF16),
        vmem((CHUNKS, ZS, tile, LANES), BF16),
        vmem((CHUNKS, ZS, tile, LANES), BF16),
        vmem((pairs, tile, LANES), BF16),
        vmem((tensors, rows, 2 * head), BF16),
        vmem((tensors, rows, 2 * head), BF16),
        dma((4 + 2 * per_holder,)),
        dma((7,)),
        dma((R_TOK + 5 * CHUNKS,)),
    ]
    return pl.pallas_call(
        functools.partial(kernel, holders, tensors),
        out_shape=(
            vmem((rows, features), BF16),
            vmem((rows, head), BF16),
            vmem((rows, head), BF16),
        ),
        in_specs=[pl.BlockSpec(memory_space=pltpu.HBM)] * 6,
        out_specs=tuple([pl.BlockSpec(memory_space=vmem)] * 3),
        scratch_shapes=scratch,
        compiler_params=pltpu.CompilerParams(
            collective_id=0, has_side_effects=True, vmem_limit_bytes=24 << 20
        ),
        name="adapters",
    )(
        *[
            pltpu.with_memory_space_constraint(operand, pltpu.HBM)
            for operand in (tokens, index.reshape(1, rows), kv_weight, down, up_query, up_value)
        ]
    )


def hand_over(*refs):
    count = len(refs) // 2
    copies = [
        pltpu.make_async_copy(refs[i], refs[count + i], refs[-1].at[i]) for i in range(count)
    ]
    for copy in copies:
        copy.start()
    for copy in copies:
        copy.wait()


def local(holders, tensors, *operands):
    outs = step(holders, tensors, *operands)
    return pl.pallas_call(
        hand_over,
        out_shape=tuple(jax.ShapeDtypeStruct(o.shape, o.dtype) for o in outs),
        in_specs=[pl.BlockSpec(memory_space=pltpu.VMEM)] * len(outs),
        out_specs=tuple([pl.BlockSpec(memory_space=pltpu.HBM)] * len(outs)),
        scratch_shapes=[pltpu.SemaphoreType.DMA((len(outs),))],
        compiler_params=pltpu.CompilerParams(vmem_limit_bytes=2 << 20),
        name="hand_over",
    )(*outs)


def solution(mesh):
    placed = (
        P("adapter", "tensor"),
        P("adapter", None),
        P("tensor", None, None),
        P("adapter", "tensor", None),
        P("adapter", None, "tensor"),
        P("adapter", None, "tensor"),
    )
    return jax.shard_map(
        functools.partial(local, mesh.shape["adapter"], mesh.shape["tensor"]),
        mesh=mesh,
        in_specs=placed,
        out_specs=(P("adapter", "tensor"), P("adapter", "tensor"), P("adapter", "tensor")),
        check_vma=False,
    )
```

time: 65.7 us -> 61.7 us (0.939)
  Pallas kernels: 64.9 us -> 60.9 us
    pallas_call x1, Pallas kernels: 63.2 us -> 60.2 us  [step(): pl.pallas_call(functools.partial(kernel, holders, tensors), out_shape=(vm...]
    pallas_call x1, Pallas kernels: 1.7 us -> 0.74 us  [local(): pl.pallas_call(hand_over, out_shape=tuple((jax.ShapeDtypeStruct(o.shape,...]
where the time goes in v3:
time: 61.7 us; the launch traced here: 61.6 us
  Pallas kernels  60.9 us (99%)
  between operations  0.64 us (1%)
    pallas_call x1, Pallas kernels, step(): pl.pallas_call(functools.partial(kernel, holders, tensors), out_shape=(vm...  60.2 us

profile of v3, /device:TPU:1, one launch (start us, length us, event | category | flops | bytes accessed | tf_op | source)
XLA Modules:
  0.0 61.6 jit_solution(12253424204466537587)
XLA Ops:
  0.6 60.2 %adapters.1 = (bf16[128,1024]{1,0:T(8,128)(2,1)S(1)}, bf16[128,128]{1,0:T(8,128)(2,1)S(1)}, bf16[128,128]{1,0:T(8,128)(2,1)S(1)}) custom-call(bf16[128,1024]{1,0:T(8,128)(2,1)} %tok_hbm.1, s32[1,128]{1,0:T(1,128)} %bitcast.1, bf16[1024,2,1024]{2,1,0:T(2,128)(2,1)} %kvw_hbm.1, bf16[2,1024,128]{2,1,0:T(8,128)(2,1)} %down_hbm.1, bf16[2,64,1024]{2,1,0:T(8,128)(2,1)} %upq_hbm.1, ...), custom_call_target="tpu_custom_call" | custom-call | tf_op jit(solution)/shard_map/adapters/pallas_call | solution.py:464
  60.8 0.7 %hand_over.1 = (bf16[128,1024]{1,0:T(8,128)(2,1)}, bf16[128,128]{1,0:T(8,128)(2,1)}, bf16[128,128]{1,0:T(8,128)(2,1)}) custom-call(bf16[128,1024]{1,0:T(8,128)(2,1)S(1)} %get-tuple-element.6.refs_0_, bf16[128,128]{1,0:T(8,128)(2,1)S(1)} %get-tuple-element.7.refs_1_, bf16[128,128]{1,0:T(8,128)(2,1)S(1)} %get-tuple-element.8.refs_2_), custom_call_target="tpu_custom_call" | custom-call | tf_op jit(solution)/shard_map/hand_over/pallas_call | solution.py:499

commit v4 on v3

--- a/solution.py
+++ b/solution.py
@@ -13,6 +13,8 @@
 MOST = 3
 ZS, XS, CORES = 8, 4, 2
 CHUNKS = XS
+Z_AWAY = (4, 3, 5, 2, 6, 1, 7, 0)
+Y_AWAY = (4, 3, 5, 2, 6, 1, 7)
 STEPS = (
     "a0", "b0", "a1", "c0", "b1", "a2", "a3", "b2", "c1", "b3", "c2", "s1", "v0", "v1", "v2",
     "c3", "v3", "f0", "f1", "f2", "base", "values", "f3",
@@ -83,18 +85,18 @@
     sibling = me + 1 - 2 * core
     self_pos = z * CORES + core
 
-    def peer_of(p):
-        offset = p // chunk
-        px = (x + offset % 2 * (1 - 2 * (x % 2)) + 2 * (offset // 2)) % XS
-        return ((p // CORES) % ZS) * (XS * CORES) + px * CORES + p % CORES
-
-    def my_pos(p):
-        return (p // chunk) * chunk + self_pos
-
-    def for_peers(k, act):
-        @pl.loop(1 if k == 0 else 0, chunk)
-        def _(d):
-            act(k * chunk + (self_pos + d) % chunk)
+    def for_peers(k, cores, act):
+        px = (x + k % 2 * (1 - 2 * (x % 2)) + 2 * (k // 2)) % XS
+        for dz in Z_AWAY:
+            pz = (z + dz) % ZS
+            for dc in cores:
+                if (k, dz, dc) != (0, 0, 0):
+                    pc = (core + dc) % CORES
+                    act(
+                        k * chunk + pz * CORES + pc,
+                        k * chunk + self_pos,
+                        (pz * XS + px) * CORES + pc,
+                    )
 
     def wait_bytes(ref, sem):
         pltpu.make_async_copy(ref, ref, sem).wait()
@@ -118,13 +120,13 @@
 
     barrier = pltpu.get_barrier_semaphore()
 
-    @pl.loop(1, tensors, unroll=7)
-    def _(d):
+    for dz in Z_AWAY:
+        for d in range(XS * CORES):
+            if (dz, d) != (0, 0):
+                to = (z + dz) % ZS * (XS * CORES) + (me + d) % (XS * CORES)
+                pl.semaphore_signal(barrier, inc=1, device_id=(to, t), device_id_type=MESH)
+    for d in Y_AWAY:
         pl.semaphore_signal(barrier, inc=1, device_id=(me, (t + d) % tensors), device_id_type=MESH)
-
-    @pl.loop(1, holders, unroll=holders - 1)
-    def _(d):
-        pl.semaphore_signal(barrier, inc=1, device_id=((me + d) % holders, t), device_id_type=MESH)
 
     get_down.start()
     get_kvw.start()
@@ -160,8 +162,9 @@
     def dispatch_chunk(k):
         for_peers(
             k,
-            lambda p: remote(
-                send.at[p], recv.at[my_pos(p)], S_TOK, R_TOK + k, (peer_of(p), t)
+            (1, 0),
+            lambda at, there, to: remote(
+                send.at[at], recv.at[there], S_TOK, R_TOK + k, (to, t)
             ).start(),
         )
 
@@ -258,8 +261,7 @@
             for m in range(MOST):
                 part[k, a * MOST + m] = terms[m * chunk : (m + 1) * chunk]
 
-        @pl.loop(1, tensors)
-        def _(d):
+        for d in Y_AWAY:
             other = (t + d) % tensors
 
             @pl.when(other < owners)
@@ -276,8 +278,7 @@
                 summed = summed + rs[k, s]
             sh[k, t] = summed.astype(BF16)
 
-            @pl.loop(1, tensors)
-            def _(d):
+            for d in Y_AWAY:
                 other = (t + d) % tensors
                 remote(sh.at[k, t], sh.at[k, t], S_SHRUNK, R_SHRUNK + k, (me, other)).start()
 
@@ -312,8 +313,9 @@
             )
         for_peers(
             k,
-            lambda p: remote(
-                ret_send.at[p], ret_recv.at[my_pos(p)], S_RET, R_RET + k, (peer_of(p), t)
+            (1, 0),
+            lambda at, there, to: remote(
+                ret_send.at[at], ret_recv.at[there], S_RET, R_RET + k, (to, t)
             ).start(),
         )
         if k == 0:
@@ -323,12 +325,13 @@
         wait_bytes(v_pair.at[k], recv_sems.at[R_PAIR + k])
         v_send[k] = v_all[k, :, core] + v_pair[k]
 
-        @pl.loop(1 if k == 0 else 0, ZS)
-        def _(d):
-            to = (z + d) % ZS
-            p = k * chunk + to * CORES + core
-            remote(v_send.at[k, to], v_recv.at[k * ZS + z], S_V, R_V, (peer_of(p), t)).start()
-
+        for_peers(
+            k,
+            (0,),
+            lambda at, there, to: remote(
+                v_send.at[k, at // CORES - k * ZS], v_recv.at[there // CORES], S_V, R_V, (to, t)
+            ).start(),
+        )
         if k == 0:
             v_recv[z] = v_send[k, z]
 

time: 61.7 us -> 59.8 us (0.969)
  Pallas kernels: 60.9 us -> 58.9 us
    pallas_call x1, Pallas kernels: 60.2 us -> 58.2 us  [step(): pl.pallas_call(functools.partial(kernel, holders, tensors), out_shape=(vm...]
where the time goes in v4:
time: 59.8 us; the launch traced here: 59.6 us
  Pallas kernels  58.9 us (98%)
  between operations  0.64 us (1%)
    pallas_call x1, Pallas kernels, step(): pl.pallas_call(functools.partial(kernel, holders, tensors), out_shape=(vm...  58.2 us

profile of v4, /device:TPU:1, one launch (start us, length us, event | category | flops | bytes accessed | tf_op | source)
XLA Modules:
  0.0 59.6 jit_solution(3523938783981957727)
XLA Ops:
  0.6 58.2 %adapters.1 = (bf16[128,1024]{1,0:T(8,128)(2,1)S(1)}, bf16[128,128]{1,0:T(8,128)(2,1)S(1)}, bf16[128,128]{1,0:T(8,128)(2,1)S(1)}) custom-call(bf16[128,1024]{1,0:T(8,128)(2,1)} %tok_hbm.1, s32[1,128]{1,0:T(1,128)} %bitcast.1, bf16[1024,2,1024]{2,1,0:T(2,128)(2,1)} %kvw_hbm.1, bf16[2,1024,128]{2,1,0:T(8,128)(2,1)} %down_hbm.1, bf16[2,64,1024]{2,1,0:T(8,128)(2,1)} %upq_hbm.1, ...), custom_call_target="tpu_custom_call" | custom-call | tf_op jit(solution)/shard_map/adapters/pallas_call | solution.py:467
  58.8 0.7 %hand_over.1 = (bf16[128,1024]{1,0:T(8,128)(2,1)}, bf16[128,128]{1,0:T(8,128)(2,1)}, bf16[128,128]{1,0:T(8,128)(2,1)}) custom-call(bf16[128,1024]{1,0:T(8,128)(2,1)S(1)} %get-tuple-element.6.refs_0_, bf16[128,128]{1,0:T(8,128)(2,1)S(1)} %get-tuple-element.7.refs_1_, bf16[128,128]{1,0:T(8,128)(2,1)S(1)} %get-tuple-element.8.refs_2_), custom_call_target="tpu_custom_call" | custom-call | tf_op jit(solution)/shard_map/hand_over/pallas_call | solution.py:502

commit v5 on v4

--- a/solution.py
+++ b/solution.py
@@ -144,18 +144,26 @@
     ordinal = jnp.dot(
         picked.astype(BF16), earlier.astype(F32).astype(BF16), preferred_element_type=F32
     )
-    get_tok.wait()
     for m in range(MOST):
         chosen = jnp.where(ordinal == float(m), picked, 0.0)
         fsel[:, m * chunk_adapters : (m + 1) * chunk_adapters, :] = chosen.reshape(
             CHUNKS, chunk_adapters, rows
         )
-        gathered = jnp.dot(chosen.astype(BF16), tok[...], preferred_element_type=F32)
-        for j in range(blocks):
-            stage[m, pl.ds(j, adapters, stride=blocks), :] = gathered[:, j * LANES : (j + 1) * LANES]
-        send[:, :, m * LANES : (m + 1) * LANES] = (
-            stage[m].reshape(holders, tile, LANES).astype(BF16)
-        )
+
+    def gather_chunk(k):
+        gathered = jnp.dot(fsel[k].astype(BF16), tok[...], preferred_element_type=F32)
+        for m in range(MOST):
+            of_m = gathered[m * chunk_adapters : (m + 1) * chunk_adapters]
+            for j in range(blocks):
+                stage[m, pl.ds(j, chunk_adapters, stride=blocks), :] = of_m[
+                    :, j * LANES : (j + 1) * LANES
+                ]
+            send[k * chunk : (k + 1) * chunk, :, m * LANES : (m + 1) * LANES] = (
+                stage[m, pl.ds(0, chunk * tile), :].reshape(chunk, tile, LANES).astype(BF16)
+            )
+
+    get_tok.wait()
+    gather_chunk(0)
 
     pl.semaphore_wait(barrier, tensors - 1 + holders - 1)
 
@@ -198,6 +206,7 @@
             lhs[c, :, 2 * j * LANES : 2 * (j + 1) * LANES] = jnp.dot(
                 tok[:, j * LANES : (j + 1) * LANES], spread, preferred_element_type=F32
             ).astype(BF16)
+    gather_chunk(1)
     dispatch_chunk(1)
     get_kvw.wait()
     run = 32
@@ -208,6 +217,7 @@
             2 * run, wbase.shape[1]
         )
 
+    gather_chunk(2)
     dispatch_chunk(2)
     @pl.loop(0, tensors // 2)
     def _(n):
@@ -219,6 +229,7 @@
                     :, half * LANES : (half + 1) * LANES
                 ]
 
+    gather_chunk(3)
     dispatch_chunk(3)
 
     def base_sends(ds):

time: 59.8 us -> 59.9 us (level)
  no operation moved by 1% of the time
where the time goes in v5:
time: 59.9 us; the launch traced here: 59.7 us
  Pallas kernels  59.1 us (99%)
  between operations  0.64 us (1%)
    pallas_call x1, Pallas kernels, step(): pl.pallas_call(functools.partial(kernel, holders, tensors), out_shape=(vm...  58.3 us

profile of v5, /device:TPU:1, one launch (start us, length us, event | category | flops | bytes accessed | tf_op | source)
XLA Modules:
  0.0 59.7 jit_solution(15760944762939208907)
XLA Ops:
  0.6 58.3 %adapters.1 = (bf16[128,1024]{1,0:T(8,128)(2,1)S(1)}, bf16[128,128]{1,0:T(8,128)(2,1)S(1)}, bf16[128,128]{1,0:T(8,128)(2,1)S(1)}) custom-call(bf16[128,1024]{1,0:T(8,128)(2,1)} %tok_hbm.1, s32[1,128]{1,0:T(1,128)} %bitcast.1, bf16[1024,2,1024]{2,1,0:T(2,128)(2,1)} %kvw_hbm.1, bf16[2,1024,128]{2,1,0:T(8,128)(2,1)} %down_hbm.1, bf16[2,64,1024]{2,1,0:T(8,128)(2,1)} %upq_hbm.1, ...), custom_call_target="tpu_custom_call" | custom-call | tf_op jit(solution)/shard_map/adapters/pallas_call | solution.py:478
  59.0 0.7 %hand_over.1 = (bf16[128,1024]{1,0:T(8,128)(2,1)}, bf16[128,128]{1,0:T(8,128)(2,1)}, bf16[128,128]{1,0:T(8,128)(2,1)}) custom-call(bf16[128,1024]{1,0:T(8,128)(2,1)S(1)} %get-tuple-element.6.refs_0_, bf16[128,128]{1,0:T(8,128)(2,1)S(1)} %get-tuple-element.7.refs_1_, bf16[128,128]{1,0:T(8,128)(2,1)S(1)} %get-tuple-element.8.refs_2_), custom_call_target="tpu_custom_call" | custom-call | tf_op jit(solution)/shard_map/hand_over/pallas_call | solution.py:513

commit v6 on v5

--- a/solution.py
+++ b/solution.py
@@ -16,9 +16,10 @@
 Z_AWAY = (4, 3, 5, 2, 6, 1, 7, 0)
 Y_AWAY = (4, 3, 5, 2, 6, 1, 7)
 STEPS = (
-    "a0", "b0", "a1", "c0", "b1", "a2", "a3", "b2", "c1", "b3", "c2", "s1", "v0", "v1", "v2",
-    "c3", "v3", "f0", "f1", "f2", "base", "values", "f3",
+    "a0", "b0", "a1", "c0", "b1", "a2", "a3", "b2", "c1", "b3", "c2", "s1", "v0", "v1", "c3",
+    "w2", "w3", "f0", "f1", "f2", "base", "values", "f3",
 )
+LATE = (2, 3)
 BASE_TO = ((1, 7), (2, 6, 3, 5, 4))
 R_BASE, R_V, R_TOK = 0, 1, 2
 R_SUM, R_SHRUNK, R_RET, R_PAIR = (R_TOK + i * CHUNKS for i in range(1, 5))
@@ -322,6 +323,8 @@
             ret_send[pl.ds(k * chunk, chunk), :, m * LANES : (m + 1) * LANES] = (
                 ustage[m].reshape(chunk, tile, LANES).astype(BF16)
             )
+        if k in LATE:
+            pl.when(core == 0)(lambda: value_tiles(k))
         for_peers(
             k,
             (1, 0),
@@ -404,6 +407,7 @@
                 "b": total,
                 "c": corrections,
                 "v": value_tiles,
+                "w": lambda k: pl.when(core == 1)(lambda: value_tiles(k)),
                 "f": select_back,
                 "s": lambda k: base_sends(BASE_TO[k]),
             }

time: 59.9 us -> 59.7 us (level)
  no operation moved by 1% of the time
where the time goes in v6:
time: 59.7 us; the launch traced here: 59.5 us
  Pallas kernels  58.9 us (99%)
  between operations  0.64 us (1%)
    pallas_call x1, Pallas kernels, step(): pl.pallas_call(functools.partial(kernel, holders, tensors), out_shape=(vm...  58.2 us

profile of v6, /device:TPU:1, one launch (start us, length us, event | category | flops | bytes accessed | tf_op | source)
XLA Modules:
  0.0 59.5 jit_solution(9374461404559978314)
XLA Ops:
  0.6 58.2 %adapters.1 = (bf16[128,1024]{1,0:T(8,128)(2,1)S(1)}, bf16[128,128]{1,0:T(8,128)(2,1)S(1)}, bf16[128,128]{1,0:T(8,128)(2,1)S(1)}) custom-call(bf16[128,1024]{1,0:T(8,128)(2,1)} %tok_hbm.1, s32[1,128]{1,0:T(1,128)} %bitcast.1, bf16[1024,2,1024]{2,1,0:T(2,128)(2,1)} %kvw_hbm.1, bf16[2,1024,128]{2,1,0:T(8,128)(2,1)} %down_hbm.1, bf16[2,64,1024]{2,1,0:T(8,128)(2,1)} %upq_hbm.1, ...), custom_call_target="tpu_custom_call" | custom-call | tf_op jit(solution)/shard_map/adapters/pallas_call | solution.py:482
  58.8 0.7 %hand_over.1 = (bf16[128,1024]{1,0:T(8,128)(2,1)}, bf16[128,128]{1,0:T(8,128)(2,1)}, bf16[128,128]{1,0:T(8,128)(2,1)}) custom-call(bf16[128,1024]{1,0:T(8,128)(2,1)S(1)} %get-tuple-element.6.refs_0_, bf16[128,128]{1,0:T(8,128)(2,1)S(1)} %get-tuple-element.7.refs_1_, bf16[128,128]{1,0:T(8,128)(2,1)S(1)} %get-tuple-element.8.refs_2_), custom_call_target="tpu_custom_call" | custom-call | tf_op jit(solution)/shard_map/hand_over/pallas_call | solution.py:517
